TPU v7x, 32 devices: a whole 2x2x4 slice. The times are simulated.
32 devices in a mesh: row: 4 (over y, x), col: 4 (over z), rep: 2 (over core).
Axes of the slice: x: 2, y: 2, z: 4, core: 2. Of those that a mesh axis runs over, the one named last changes fastest.
Arguments:
- features: bfloat16 [2, 2048, 512], P('rep', ('row', 'col')), may hold values from -6 to 6
- cotangent: bfloat16 [2, 2048, 512], P('rep', ('row', 'col')), may hold values from -6 to 6
- weight: bfloat16 [512, 512], replicated, may hold values from -0.25 to 0.25
- tile_values: bfloat16 [2, 256, 128, 128], P('rep', ('row', 'col')), may hold values from -0.25 to 0.25
- tile_out: int32 [2, 256], P('rep', ('row', 'col')), may hold values from 0 to 3
- tile_in: int32 [2, 256], P('rep', ('row', 'col')), may hold values from 0 to 3
- tile_count: int32 [2, 16], P('rep', ('row', 'col')), may hold values from 8 to 16, as said below
Outputs:
- out_feats: bfloat16 [2, 2048, 512], P('rep', ('row', 'col'))
- grad_feats: bfloat16 [2, 2048, 512], P('rep', ('row', 'col'))
- grad_weight: float32 [512, 512], replicated
Inputs may be any that keep to these rules, and one draw needn't show every extreme that they name: `tile_count`: in each window some group has all 16 slots live.
All inputs are finite; a program needn't handle non-finite values.
Results may differ from a plain program's by a relative error of at most 0.015.
Values may be sent and summed in bfloat16 or wider, within the bound.
A program may use at most 64 MiB of HBM per device.

v0:
```python
import jax
import jax.numpy as jnp
from jax import lax
from jax.sharding import PartitionSpec as P

SECTIONS = 4


def passed_along(value, axis, steps):
    count = lax.axis_size(axis)
    leading, last = (max(0, -steps), min(count, count - steps))
    return lax.ppermute(value, axis, [(source, source + steps) for source in range(leading, last)])


def body(features, cotangent, weight, tile_values, tile_out, tile_in, tile_count):
    field_in = features[0]
    values = tile_values[0]
    outs_idx = tile_out[0]
    ins_idx = tile_in[0]
    count = tile_count[0, 0]
    node_rows, width = field_in.shape
    edge = values.shape[-1]
    per_span = node_rows // edge
    half = SECTIONS // 2
    col_count = lax.axis_size("col")
    out_count = col_count * per_span
    in_count = SECTIONS * per_span
    slot_total = values.shape[0]
    live = (jnp.arange(slot_total, dtype=jnp.int32) < count).astype(jnp.float32)
    out_hot = (outs_idx[None, :] == jnp.arange(out_count, dtype=jnp.int32)[:, None]).astype(
        jnp.float32
    ) * live[None, :]
    in_hot = (ins_idx[None, :] == jnp.arange(in_count, dtype=jnp.int32)[:, None]).astype(
        jnp.float32
    ) * live[None, :]
    pieces = []
    for section in range(SECTIONS):
        offset = section - half
        if offset == 0:
            pieces.append(field_in)
        else:
            pieces.append(passed_along(field_in, "row", -offset))
    blocks = jnp.stack(pieces)
    picked = blocks[ins_idx]
    prods = jnp.einsum("tij,tjf->tif", values, picked, preferred_element_type=jnp.float32)
    part = jnp.einsum("ot,tif->oif", out_hot, prods, precision=lax.Precision.HIGHEST)
    summed = lax.psum_scatter(
        part.reshape(out_count * edge, width).astype(jnp.bfloat16),
        "col",
        scatter_dimension=0,
        tiled=True,
    )
    pre = jnp.dot(summed, weight, preferred_element_type=jnp.float32)
    out_feats = jax.nn.silu(pre).astype(jnp.bfloat16)
    sigma = jax.nn.sigmoid(pre)
    dpre = (cotangent[0].astype(jnp.float32) * sigma * (1.0 + pre * (1.0 - sigma))).astype(
        jnp.bfloat16
    )
    local_grad = jnp.einsum("nf,ng->fg", summed, dpre, preferred_element_type=jnp.float32)
    total_nodes = node_rows * lax.axis_size("row") * col_count * lax.axis_size("rep")
    grad_weight = lax.psum(local_grad, ("row", "col", "rep")) * jnp.float32(total_nodes) ** (-0.5)
    dhidden = jnp.einsum("nf,gf->ng", dpre, weight, preferred_element_type=jnp.float32).astype(
        jnp.bfloat16
    )
    row_grads = lax.all_gather(dhidden, "col", axis=0, tiled=True).reshape(out_count, edge, width)
    chosen = row_grads[outs_idx]
    back_prods = jnp.einsum("tij,tif->tjf", values, chosen, preferred_element_type=jnp.float32)
    sections_part = jnp.einsum("it,tjf->ijf", in_hot, back_prods, precision=lax.Precision.HIGHEST)
    sections_part = sections_part.astype(jnp.bfloat16)
    total = jnp.zeros((node_rows, width), jnp.float32)
    for section in range(SECTIONS):
        offset = section - half
        if offset == 0:
            arrived = sections_part[section]
        else:
            arrived = passed_along(sections_part[section], "row", offset)
        total = total + arrived.astype(jnp.float32)
    grad_feats = total.astype(jnp.bfloat16)
    return (out_feats[None], grad_feats[None], grad_weight)


def solution(mesh):
    return jax.shard_map(
        body,
        mesh=mesh,
        in_specs=(
            P("rep", ("row", "col"), None),
            P("rep", ("row", "col"), None),
            P(),
            P("rep", ("row", "col"), None, None),
            P("rep", ("row", "col")),
            P("rep", ("row", "col")),
            P("rep", ("row", "col")),
        ),
        out_specs=(P("rep", ("row", "col"), None), P("rep", ("row", "col"), None), P()),
        check_vma=False,
    )
```

profile of v0, /device:TPU:1, one launch (start us, length us, event | category | flops | bytes accessed | tf_op | source)
XLA Modules:
  0.0 223.0 jit_solution(10835809086337116893)
XLA Ops:
  7.2 4.1 %collective-permute-start = (bf16[128,512]{1,0:T(8,128)(2,1)}, bf16[128,512]{1,0:T(8,128)(2,1)S(1)}, u32[]{:S(2)}, u32[]{:S(2)}) collective-permute-start(bf16[128,512]{1,0:T(8,128)(2,1)} %bitcast.76), channel_id=1, source_target_pairs={{0,16},{8,24},{1,17},{9,25},{2,18},{10,26},{3,19},{11,27},{4,20},{... | collective-permute-start | bytes 393224 | tf_op jit(solution)/shard_map/ppermute | solution.py:12
  11.3 3.1 %collective-permute-start.1 = (bf16[128,512]{1,0:T(8,128)(2,1)}, bf16[128,512]{1,0:T(8,128)(2,1)S(1)}, u32[]{:S(2)}, u32[]{:S(2)}) collective-permute-start(bf16[128,512]{1,0:T(8,128)(2,1)} %bitcast.77), channel_id=1, source_target_pairs={{0,8},{8,16},{16,24},{1,9},{9,17},{17,25},{2,10},{10,18},{18,26},{... | collective-permute-start | bytes 393224 | tf_op jit(solution)/shard_map/ppermute | solution.py:12
  14.5 1.3 collective-permute-start.2
  17.1 3.3 %collective-permute-done.2 = bf16[128,512]{1,0:T(8,128)(2,1)S(1)} collective-permute-done((bf16[128,512]{1,0:T(8,128)(2,1)}, bf16[128,512]{1,0:T(8,128)(2,1)S(1)}, u32[]{:S(2)}, u32[]{:S(2)}) %collective-permute-start.2) | collective-permute-done | bytes 131104 | tf_op jit(solution)/shard_map/ppermute | solution.py:12
  20.4 1.0 pad_maximum_fusion
  22.1 2.7 %fusion.12 = f32[16,512,128]{2,1,0:T(8,128)} fusion(bf16[16,128,512]{2,1,0:T(8,128)(2,1)S(1)} %gather_fusion, bf16[1,16,128,128]{3,2,1,0:T(8,128)(2,1)S(1)} %copy-done), kind=kOutput, calls=%fused_computation.12 | convolution fusion | flops 268435456 | bytes 6815744 | tf_op jit(solution)/shard_map/tij,tjf->tif/dot_general | solution.py:45
  24.8 5.5 %copy.16 = f32[16,512,128]{1,0,2:T(8,128)} copy(f32[16,512,128]{2,1,0:T(8,128)} %fusion.12) | data formatting | bytes 8388608 | tf_op jit(solution)/shard_map/tij,tjf->tif/dot_general | solution.py:45
  30.3 4.3 %fusion.4 = bf16[4,128,512]{2,0,1:T(4,128)(2,1)S(1)} fusion(f32[16,512,128]{1,0,2:T(8,128)} %copy.16, f32[16]{0:T(128)S(1)} %compare_convert_fusion, s32[16]{0:T(128)S(1)} %bitcast.82), kind=kOutput, calls=%fused_computation.6 | convolution fusion | flops 50593920 | bytes 4718720 | tf_op jit(solution)/shard_map/ot,tif->oif/dot_general | solution.py:46
  34.7 0.9 copy.13
  35.7 21.4 %reduce-scatter.2.cloned.1.call-done = bf16[128,512]{1,0:T(8,128)(2,1)} async-done(((bf16[512,512]{1,0:T(8,128)(2,1)}), bf16[128,512]{1,0:T(8,128)(2,1)}) %reduce-scatter.2.cloned.1.call-update) | async-done | bytes 131088 | tf_op jit(solution)/shard_map/reduce_scatter | solution.py:47
  57.1 1.1 fusion.38
  58.6 12.9 %all_gather.3 = bf16[512,512]{1,0:T(8,128)(2,1)S(1)} all-gather(bf16[128,512]{1,0:T(8,128)(2,1)S(1)} %convolution_convert_fusion), channel_id=1, replica_groups=mesh['row'=4,'col'=4,'rep'=2] {'col'}, dimensions={0}, use_global_device_ids=true | all-gather | bytes 655360 | tf_op jit(solution)/shard_map/all_gather | solution.py:65
  72.2 2.8 %fusion.10 = f32[16,512,128]{2,1,0:T(8,128)} fusion(bf16[16,128,512]{2,1,0:T(8,128)(2,1)S(1)} %gather_fusion.1, bf16[1,16,128,128]{3,2,1,0:T(8,128)(2,1)S(1)} %copy-done), kind=kOutput, calls=%fused_computation.10 | convolution fusion | flops 268435456 | bytes 6815744 | tf_op jit(solution)/shard_map/tij,tif->tjf/dot_general | solution.py:67
  74.9 5.5 %copy.17 = f32[16,512,128]{1,0,2:T(8,128)} copy(f32[16,512,128]{2,1,0:T(8,128)} %fusion.10) | data formatting | bytes 8388608 | tf_op jit(solution)/shard_map/tij,tif->tjf/dot_general | solution.py:67
  80.5 1.4 fusion.34
  81.9 4.3 %fusion.7 = bf16[4,128,512]{2,0,1:T(4,128)(2,1)S(1)} fusion(f32[16,512,128]{1,0,2:T(8,128)} %copy.17, s32[16]{0:T(128)S(1)} %bitcast.83, f32[16]{0:T(128)S(1)} %compare_convert_fusion), kind=kOutput, calls=%fused_computation.7 | convolution fusion | flops 50593920 | bytes 4718720 | tf_op jit(solution)/shard_map/it,tjf->ijf/dot_general | solution.py:68
  86.1 0.7 fusion.37
  86.9 1.3 collective-permute-start.3
  88.2 1.3 collective-permute-start.4
  89.6 4.0 %collective-permute-start.5 = (bf16[128,512]{1,0:T(8,128)(2,1)S(1)}, bf16[128,512]{1,0:T(8,128)(2,1)S(1)}, u32[]{:S(2)}, u32[]{:S(2)}) collective-permute-start(bf16[128,512]{1,0:T(8,128)(2,1)S(1)} %bitcast.75), channel_id=1, source_target_pairs={{0,8},{8,16},{16,24},{1,9},{9,17},{17,25},{2,10},{10,18},{18,26},{... | collective-permute-start | bytes 393224 | tf_op jit(solution)/shard_map/ppermute | solution.py:12
  93.6 0.7 fusion.19
  94.4 1.4 collective-permute-done.5
  96.5 117.3 %all-reduce.2.cloned.1.call-done = f32[512,512]{1,0:T(8,128)} async-done(((f32[512,512]{1,0:T(8,128)}), f32[512,512]{1,0:T(8,128)}) %all-reduce.2.cloned.1.call-update) | async-done | bytes 1048592 | tf_op jit(solution)/shard_map/psum | solution.py:61
  213.9 2.3 %broadcast_multiply_fusion = f32[512,512]{1,0:T(8,128)} fusion(f32[512,512]{1,0:T(8,128)} %all-reduce.2.cloned.1.call-done), kind=kLoop, calls=%fused_computation.14 | loop fusion | flops 262144 | bytes 2097152 | tf_op jit(solution)/shard_map/mul | solution.py:61
  (32 shorter events, 3.3 us)
Async XLA Ops:
  7.2 14.9 %copy-start = (bf16[1,16,128,128]{3,2,1,0:T(8,128)(2,1)S(1)}, bf16[1,16,128,128]{3,2,1,0:T(8,128)(2,1)}, u32[]{:S(2)}) copy-start(bf16[1,16,128,128]{3,2,1,0:T(8,128)(2,1)} %param.10) | copy-start | bytes 1572868
  7.2 49.9 %reduce-scatter.2.cloned.1.call-start = ((), (), s32[]{:S(2)}) async-start(), calls=%async_computation.1 | async-start | bytes 655360 | tf_op jit(solution)/shard_map/reduce_scatter | solution.py:47
  7.2 9.9 %collective-permute-start = (bf16[128,512]{1,0:T(8,128)(2,1)}, bf16[128,512]{1,0:T(8,128)(2,1)S(1)}, u32[]{:S(2)}, u32[]{:S(2)}) collective-permute-start(bf16[128,512]{1,0:T(8,128)(2,1)} %bitcast.76), channel_id=1, source_target_pairs={{0,16},{8,24},{1,17},{9,25},{2,18},{10,26},{3,19},{11,27},{4,20},{... | collective-permute-start | bytes 393224 | tf_op jit(solution)/shard_map/ppermute | solution.py:12
  11.3 5.8 %collective-permute-start.1 = (bf16[128,512]{1,0:T(8,128)(2,1)}, bf16[128,512]{1,0:T(8,128)(2,1)S(1)}, u32[]{:S(2)}, u32[]{:S(2)}) collective-permute-start(bf16[128,512]{1,0:T(8,128)(2,1)} %bitcast.77), channel_id=1, source_target_pairs={{0,8},{8,16},{16,24},{1,9},{9,17},{17,25},{2,10},{10,18},{18,26},{... | collective-permute-start | bytes 393224 | tf_op jit(solution)/shard_map/ppermute | solution.py:12
  14.5 5.9 %collective-permute-start.2 = (bf16[128,512]{1,0:T(8,128)(2,1)}, bf16[128,512]{1,0:T(8,128)(2,1)S(1)}, u32[]{:S(2)}, u32[]{:S(2)}) collective-permute-start(bf16[128,512]{1,0:T(8,128)(2,1)} %bitcast.78), channel_id=1, source_target_pairs={{8,0},{16,8},{24,16},{9,1},{17,9},{25,17},{10,2},{18,10},{26,18},{... | collective-permute-start | bytes 393224 | tf_op jit(solution)/shard_map/ppermute | solution.py:12
  24.8 5.5 %copy-start.3 = (s32[1,16]{1,0:T(1,128)S(1)}, s32[1,16]{1,0:T(1,128)}, u32[]{:S(2)}) copy-start(s32[1,16]{1,0:T(1,128)} %param.11) | copy-start | bytes 196
  30.3 26.8 %copy-start.1 = (bf16[512,512]{1,0:T(8,128)(2,1)S(1)}, bf16[512,512]{1,0:T(8,128)(2,1)}, u32[]{:S(2)}) copy-start(bf16[512,512]{1,0:T(8,128)(2,1)} %param.9) | copy-start | bytes 1572868
  34.7 23.6 %copy-start.5 = (bf16[1,128,512]{2,1,0:T(8,128)(2,1)S(1)}, bf16[1,128,512]{2,1,0:T(8,128)(2,1)}, u32[]{:S(2)}) copy-start(bf16[1,128,512]{2,1,0:T(8,128)(2,1)} %param.8) | copy-start | bytes 393220
  35.6 178.3 %all-reduce.2.cloned.1.call-start = ((), (), s32[]{:S(2)}) async-start(), calls=%async_computation.2 | async-start | bytes 2097152 | tf_op jit(solution)/shard_map/psum | solution.py:61
  74.9 5.5 %copy-start.2 = (bf16[128,512]{1,0:T(8,128)(2,1)S(1)}, bf16[128,512]{1,0:T(8,128)(2,1)}, u32[]{:S(2)}) copy-start(bf16[128,512]{1,0:T(8,128)(2,1)} %reduce-scatter.2.cloned.1.call-done) | copy-start | bytes 393220
  80.5 1.4 copy-start.4
  86.9 7.4 %collective-permute-start.3 = (bf16[128,512]{1,0:T(8,128)(2,1)S(1)}, bf16[128,512]{1,0:T(8,128)(2,1)S(1)}, u32[]{:S(2)}, u32[]{:S(2)}) collective-permute-start(bf16[128,512]{1,0:T(8,128)(2,1)S(1)} %bitcast.73), channel_id=1, source_target_pairs={{16,0},{24,8},{17,1},{25,9},{18,2},{26,10},{19,3},{27,11},{20,4},{... | collective-permute-start | bytes 393224 | tf_op jit(solution)/shard_map/ppermute | solution.py:12
  88.2 6.1 %collective-permute-start.4 = (bf16[128,512]{1,0:T(8,128)(2,1)S(1)}, bf16[128,512]{1,0:T(8,128)(2,1)S(1)}, u32[]{:S(2)}, u32[]{:S(2)}) collective-permute-start(bf16[128,512]{1,0:T(8,128)(2,1)S(1)} %bitcast.74), channel_id=1, source_target_pairs={{8,0},{16,8},{24,16},{9,1},{17,9},{25,17},{10,2},{18,10},{26,18},{... | collective-permute-start | bytes 393224 | tf_op jit(solution)/shard_map/ppermute | solution.py:12
  89.6 6.2 %collective-permute-start.5 = (bf16[128,512]{1,0:T(8,128)(2,1)S(1)}, bf16[128,512]{1,0:T(8,128)(2,1)S(1)}, u32[]{:S(2)}, u32[]{:S(2)}) collective-permute-start(bf16[128,512]{1,0:T(8,128)(2,1)S(1)} %bitcast.75), channel_id=1, source_target_pairs={{0,8},{8,16},{16,24},{1,9},{9,17},{17,25},{2,10},{10,18},{18,26},{... | collective-permute-start | bytes 393224 | tf_op jit(solution)/shard_map/ppermute | solution.py:12
Sparse Core Ops, SparseCore 0:
  35.7 21.3 reduce-scatter.1
  82.0 131.8 all-reduce.1
where the time goes:
time: 225 us; the launch traced here: 223 us
  waiting for transfers between devices  144 us (64%)
  matrix products  16.9 us (8%)
  starting transfers between devices  15.2 us (7%)
  between operations  14.9 us (7%)
  local copies, waits for them, and re-layouts  13.4 us (6%)
  blocking collectives  12.9 us (6%)
  other arithmetic  6.11 us (3%)
    psum x1, waiting for transfers between devices, body(): lax.psum(local_grad, ('row', 'col', 'rep'))  117 us
    reduce_scatter x1, waiting for transfers between devices, body(): lax.psum_scatter(part.reshape(out_count * edge, width).astype(jnp.bfloat1...  21.4 us
    ppermute x6, starting transfers between devices, passed_along(): lax.ppermute(value, axis, [(source, source + steps) for source in range(l...  15.1 us
    all_gather x1, blocking collectives, body(): lax.all_gather(dhidden, 'col', axis=0, tiled=True)  12.9 us
    dot_general x1, local copies, waits for them, and re-layouts, body(): jnp.einsum('tij,tif->tjf', values, chosen, preferred_element_type=jnp.flo...  5.54 us
    dot_general x1, local copies, waits for them, and re-layouts, body(): jnp.einsum('tij,tjf->tif', values, picked, preferred_element_type=jnp.flo...  5.51 us
    ppermute x6, waiting for transfers between devices, passed_along(): lax.ppermute(value, axis, [(source, source + steps) for source in range(l...  4.78 us
  transfers between devices with their start and end apart: 8, of which 5 were waited for; matrix products, arithmetic and copies ran while one was open for 3% of the time, Pallas kernels for 0%

commit v1 on v0

v1 whole, which is shorter than its diff:
```python
import functools

import jax
import jax.numpy as jnp
from jax import lax
from jax.experimental import pallas as pl
from jax.experimental.pallas import tpu as pltpu
from jax.sharding import PartitionSpec as P

SECTIONS = 4
HALF = SECTIONS // 2
OTHERS = tuple(s for s in range(SECTIONS) if s != HALF)
CHUNKS = 4
MESH = pl.DeviceIdType.MESH
F32, BF16 = jnp.float32, jnp.bfloat16


def remote(src, dst, send, recv, axis, index):
    return pltpu.make_async_remote_copy(
        src_ref=src, dst_ref=dst, send_sem=send, recv_sem=recv, device_id={axis: index}, device_id_type=MESH
    )


def dot(a, b, dims=((1,), (0,))):
    return lax.dot_general(a, b, (dims, ((), ())), preferred_element_type=F32)


def kernel(
    rows, cols, reps, fused,
    feat, cot, w, vals, touts, tins, tcount,
    out, gfeat, gweight,
    a, at, x, part, arrived, hid, grads, secs, landed,
    mine, rep_in, row_out, row_in, col_out, col_in, full,
    xs, xr, ps, pr, gs, gr, ss, sr, rs, rr, ws, wr, cs, cr, rs2, rr2, ws2, wr2, cs2, cr2,
):
    r, c, p = lax.axis_index("row"), lax.axis_index("col"), lax.axis_index("rep")
    span, width = feat.shape[1:]
    wide = width // CHUNKS
    edge = vals.shape[-1]
    slots = vals.shape[1]
    own = pl.ds(pl.multiple_of(c * span, span), span)

    def sec(s):
        return pl.ds(s * span, span)

    def cut(j):
        return pl.ds(j * wide, wide)

    def inside(index):
        return jnp.logical_and(index >= 0, index < rows)

    def ring(axis, me, count):
        return [(k - 1, axis, lax.rem(me + k, count)) for k in range(1, count)]

    col_peers = ring("col", c, cols)
    row_peers = ring("row", r, rows) if fused else []
    rep_peers = ring("rep", p, reps) if fused else []

    barrier = pltpu.get_barrier_semaphore()
    for _, axis, index in col_peers + row_peers + rep_peers:
        pl.semaphore_signal(barrier, inc=1, device_id={axis: index}, device_id_type=MESH)
    if not fused:
        for d in (-2, -1, 1, 2):
            @pl.when(inside(r + d))
            def _():
                pl.semaphore_signal(barrier, inc=1, device_id={"row": r + d}, device_id_type=MESH)
        for d in (-2, -1, 1, 2):
            @pl.when(inside(r + d))
            def _():
                pl.semaphore_wait(barrier, 1)
    pl.semaphore_wait(barrier, len(col_peers + row_peers + rep_peers))

    def x_copy(j, n, s):
        return remote(feat.at[0, :, cut(j)], x.at[j, sec(s), :], xs.at[j, n], xr.at[j, n], "row", r - (s - HALF))

    for j in range(CHUNKS):
        for n, s in enumerate(OTHERS):
            @pl.when(inside(r - (s - HALF)))
            def _():
                x_copy(j, n, s).start()

    for j in range(CHUNKS):
        x[j, sec(HALF), :] = feat[0, :, j * wide : (j + 1) * wide]
        for n, s in enumerate(OTHERS):
            @pl.when(jnp.logical_not(inside(r + (s - HALF))))
            def _():
                x[j, sec(s), :] = jnp.zeros((span, wide), BF16)

            @pl.when(jnp.logical_not(inside(r - (s - HALF))))
            def _():
                landed[j, n] = jnp.zeros((span, wide), BF16)

    count = tcount[0, 0]
    one, zero = jnp.float32(1), jnp.float32(0)
    hot_out = [[jnp.where(touts[0, t] == o, one, zero) for o in range(cols)] for t in range(slots)]
    hot_in = [
        [jnp.where(jnp.logical_and(tins[0, t] == i, t < count), one, zero) for i in range(SECTIONS)]
        for t in range(slots)
    ]
    strip = 16

    @pl.loop(0, edge // strip)
    def _(step):
        at_row = pl.multiple_of(step * strip, strip)
        total = [[jnp.zeros((strip, edge), F32) for _ in range(SECTIONS)] for _ in range(cols)]
        for t in range(slots):
            v = vals[0, t, pl.ds(at_row, strip), :].astype(F32)
            for i in range(SECTIONS):
                picked = v * hot_in[t][i]
                for o in range(cols):
                    total[o][i] = total[o][i] + picked * hot_out[t][o]
        for o in range(cols):
            for i in range(SECTIONS):
                a[pl.ds(o * edge + at_row, strip), i * edge : (i + 1) * edge] = total[o][i].astype(BF16)

    def part_copy(j, k, axis, index):
        rows_of = pl.ds(pl.multiple_of(index * span, span), span)
        return remote(part.at[j, rows_of, :], arrived.at[j, k], ps.at[j, k], pr.at[j, k], axis, index)

    for j in range(CHUNKS):
        for n, s in enumerate(OTHERS):
            @pl.when(inside(r + (s - HALF)))
            def _():
                x_copy(j, n, s).wait_recv()
        part[j] = dot(a[...], x[j]).astype(BF16)
        for peer in col_peers:
            part_copy(j, *peer).start()

    at[...] = a[...].astype(F32).T.astype(BF16)

    pre = jnp.zeros((span, width), F32)
    for j in range(CHUNKS):
        for peer in col_peers:
            part_copy(j, *peer).wait_recv()
        summed = part[j, own, :].astype(F32)
        for k in range(cols - 1):
            summed = summed + arrived[j, k].astype(F32)
        summed = summed.astype(BF16)
        hid[:, j * wide : (j + 1) * wide] = summed
        pre = pre + dot(summed, w[j * wide : (j + 1) * wide, :])

    sigma = jax.nn.sigmoid(pre)
    dpre = (cot[0].astype(F32) * sigma * (1.0 + pre * (1.0 - sigma))).astype(BF16)

    def grad_copy(j, k, axis, index):
        return remote(grads.at[j, own, :], grads.at[j, own, :], gs.at[j, k], gr.at[j, k], axis, index)

    def grad_wait(j, k):
        source = pl.ds(pl.multiple_of(lax.rem(c + cols - 1 - k, cols) * span, span), span)
        remote(grads.at[j, source, :], grads.at[j, source, :], gs.at[j, k], gr.at[j, k], "col", col_peers[k][2]).wait_recv()

    for j in range(CHUNKS):
        grads[j, own, :] = dot(dpre, w[j * wide : (j + 1) * wide, :], ((1,), (1,))).astype(BF16)
        for peer in col_peers:
            grad_copy(j, *peer).start()
    out[0] = (pre * sigma).astype(BF16)

    scale = float(span * rows * cols * reps) ** -0.5
    term = dot(hid[...].astype(F32).T.astype(BF16), dpre) * scale
    if not fused:
        gweight[...] = term
    else:
        mine[...] = term.astype(BF16)
        rep_rows = width // reps
        row_rows = rep_rows // rows
        col_rows = row_rows // cols

        def piece(size, index):
            return pl.ds(pl.multiple_of(index * size, size), size)

        def rep_copy(k, axis, index):
            return remote(mine.at[piece(rep_rows, index), :], rep_in.at[k], rs.at[k], rr.at[k], axis, index)

        def row_copy(k, axis, index):
            return remote(row_out.at[piece(row_rows, index), :], row_in.at[k], ws.at[k], wr.at[k], axis, index)

        def col_copy(k, axis, index):
            return remote(col_out.at[piece(col_rows, index), :], col_in.at[k], cs.at[k], cr.at[k], axis, index)

        def place(level, p, r, c):
            start = p * rep_rows
            if level < 2:
                start = start + r * row_rows
            if level < 1:
                start = start + c * col_rows
            size = (col_rows, row_rows, rep_rows)[level]
            return full.at[pl.ds(pl.multiple_of(start, size), size), :]

        def back_copy(level, k, axis, index, arriving=False):
            send, recv = ((cs2, cr2), (ws2, wr2), (rs2, rr2))[level]
            where = [p, r, c]
            if arriving:
                which = ("rep", "row", "col").index(axis)
                total = (reps, rows, cols)[which]
                where[which] = lax.rem(where[which] + total - 1 - k, total)
            spot = place(level, *where)
            return remote(spot, spot, send.at[k], recv.at[k], axis, index)

        for peer in rep_peers:
            rep_copy(*peer).start()

    def adjoint(j):
        for k in range(cols - 1):
            grad_wait(j, k)
        secs[j] = dot(at[...], grads[j]).astype(BF16)
        for n, s in enumerate(OTHERS):
            @pl.when(inside(r + (s - HALF)))
            def _():
                sec_copy(j, n, s).start()

    def sec_copy(j, n, s):
        return remote(secs.at[j, sec(s), :], landed.at[j, n], ss.at[j, n], sr.at[j, n], "row", r + (s - HALF))

    def finish(j):
        total = secs[j, sec(HALF), :].astype(F32)
        for n, s in enumerate(OTHERS):
            @pl.when(inside(r - (s - HALF)))
            def _():
                sec_copy(j, n, s).wait_recv()
        for n in range(len(OTHERS)):
            total = total + landed[j, n].astype(F32)
        gfeat[0, :, j * wide : (j + 1) * wide] = total.astype(BF16)

    def rep_stage():
        for peer in rep_peers:
            rep_copy(*peer).wait_recv()
        total = mine[piece(rep_rows, p), :].astype(F32)
        for k in range(reps - 1):
            total = total + rep_in[k].astype(F32)
        row_out[...] = total.astype(BF16)
        for peer in row_peers:
            row_copy(*peer).start()

    def row_stage():
        for peer in row_peers:
            row_copy(*peer).wait_recv()
        total = row_out[piece(row_rows, r), :].astype(F32)
        for k in range(rows - 1):
            total = total + row_in[k].astype(F32)
        col_out[...] = total.astype(BF16)
        for peer in col_peers:
            col_copy(*peer).start()

    def col_stage():
        for peer in col_peers:
            col_copy(*peer).wait_recv()
        total = col_out[piece(col_rows, c), :].astype(F32)
        for k in range(cols - 1):
            total = total + col_in[k].astype(F32)
        place(0, p, r, c)[...] = total.astype(BF16)
        for peer in col_peers:
            back_copy(0, *peer).start()

    def back_stage(level, peers, then):
        for peer in peers:
            back_copy(level, *peer, arriving=True).wait_recv()
        for peer in then:
            back_copy(level + 1, *peer).start()

    if fused:
        rep_stage()
    for j in range(CHUNKS):
        adjoint(j)
        if fused and j == CHUNKS // 2:
            row_stage()
    if fused:
        col_stage()
    for j in range(CHUNKS):
        finish(j)
        if fused and j == CHUNKS // 2:
            back_stage(0, col_peers, row_peers)
    if fused:
        back_stage(1, row_peers, rep_peers)
        back_stage(2, rep_peers, [])
        gweight[...] = full[...].astype(F32)

    for j in range(CHUNKS):
        for n, s in enumerate(OTHERS):
            @pl.when(inside(r - (s - HALF)))
            def _():
                x_copy(j, n, s).wait_send()

            @pl.when(inside(r + (s - HALF)))
            def _():
                sec_copy(j, n, s).wait_send()
        for peer in col_peers:
            part_copy(j, *peer).wait_send()
            grad_copy(j, *peer).wait_send()
    if fused:
        for peer in rep_peers:
            rep_copy(*peer).wait_send()
            back_copy(2, *peer).wait_send()
        for peer in row_peers:
            row_copy(*peer).wait_send()
            back_copy(1, *peer).wait_send()
        for peer in col_peers:
            col_copy(*peer).wait_send()
            back_copy(0, *peer).wait_send()


def solution(mesh):
    rows, cols, reps = (mesh.shape[name] for name in ("row", "col", "rep"))

    def body(feat, cot, w, vals, touts, tins, tcount):
        span, width = feat.shape[1:]
        edge = vals.shape[-1]
        wide = width // CHUNKS
        fused = width % (16 * rows * cols * reps) == 0
        rep_rows = width // reps if fused else 16
        row_rows = rep_rows // rows if fused else 16
        col_rows = row_rows // cols if fused else 16
        few = lambda n: max(1, n - 1)
        vmem = pl.BlockSpec(memory_space=pltpu.VMEM)
        smem = pl.BlockSpec(memory_space=pltpu.SMEM)
        sems = lambda *shape: [pltpu.SemaphoreType.DMA(shape)] * 2
        result = pl.pallas_call(
            functools.partial(kernel, rows, cols, reps, fused),
            out_shape=(
                jax.ShapeDtypeStruct(feat.shape, BF16),
                jax.ShapeDtypeStruct(feat.shape, BF16),
                jax.ShapeDtypeStruct(w.shape, F32),
            ),
            in_specs=[vmem] * 4 + [smem] * 3,
            out_specs=(vmem,) * 3,
            scratch_shapes=[
                pltpu.VMEM((cols * edge, SECTIONS * edge), BF16),
                pltpu.VMEM((SECTIONS * edge, cols * edge), BF16),
                pltpu.VMEM((CHUNKS, SECTIONS * span, wide), BF16),
                pltpu.VMEM((CHUNKS, cols * span, wide), BF16),
                pltpu.VMEM((CHUNKS, few(cols), span, wide), BF16),
                pltpu.VMEM((span, width), BF16),
                pltpu.VMEM((CHUNKS, cols * span, wide), BF16),
                pltpu.VMEM((CHUNKS, SECTIONS * span, wide), BF16),
                pltpu.VMEM((CHUNKS, len(OTHERS), span, wide), BF16),
                pltpu.VMEM(w.shape if fused else (16, width), BF16),
                pltpu.VMEM((few(reps), rep_rows, width), BF16),
                pltpu.VMEM((rep_rows, width), BF16),
                pltpu.VMEM((few(rows) if fused else 1, row_rows, width), BF16),
                pltpu.VMEM((row_rows, width), BF16),
                pltpu.VMEM((few(cols), col_rows, width), BF16),
                pltpu.VMEM(w.shape if fused else (16, width), BF16),
                *sems(CHUNKS, len(OTHERS)),
                *sems(CHUNKS, few(cols)),
                *sems(CHUNKS, few(cols)),
                *sems(CHUNKS, len(OTHERS)),
                *(sems(few(reps)) + sems(few(rows) if fused else 1) + sems(few(cols))) * 2,
            ],
            compiler_params=pltpu.CompilerParams(
                collective_id=0, has_side_effects=True, vmem_limit_bytes=48 * 2**20
            ),
        )(feat, cot, w, vals, touts, tins, tcount)
        if fused:
            return result
        return (*result[:2], lax.psum(result[2], ("row", "col", "rep")))

    spread = ("row", "col")
    return jax.shard_map(
        body,
        mesh=mesh,
        in_specs=(
            P("rep", spread, None), P("rep", spread, None), P(), P("rep", spread, None, None),
            P("rep", spread), P("rep", spread), P("rep", spread),
        ),
        out_specs=(P("rep", spread, None), P("rep", spread, None), P()),
        check_vma=False,
    )
```

time: 225 us -> 54.8 us (0.24)
  waiting for transfers between devices: 144 us -> 0 us
  Pallas kernels: 0 us -> 47 us
  matrix products: 16.9 us -> 0 us
  starting transfers between devices: 15.2 us -> 0 us
  between operations: 14.9 us -> 1.35 us
  blocking collectives: 12.9 us -> 0 us
  local copies, waits for them, and re-layouts: 13.4 us -> 6.17 us
  other arithmetic: 6.11 us -> 0 us
    psum x1 -> x0, waiting for transfers between devices: 117 us -> none  [body(): lax.psum(local_grad, ('row', 'col', 'rep'))]
    pallas_call x0 -> x1, Pallas kernels: none -> 47 us  [body(): pl.pallas_call(functools.partial(kernel, rows, cols, reps, fused), out_sh...]
    reduce_scatter x1 -> x0, waiting for transfers between devices: 21.4 us -> none  [body(): lax.psum_scatter(part.reshape(out_count * edge, width).astype(jnp.bfloat1...]
    dot_general x7 -> x0, matrix products: 16.9 us -> none  [the longest x1 4.33 us: body(): jnp.einsum('ot,tif->oif', out_hot, prods, precision=lax.Precision.HIGHEST)]
    ppermute x6 -> x0, starting transfers between devices: 15.1 us -> none  [passed_along(): lax.ppermute(value, axis, [(source, source + steps) for source in range(l...]
    all_gather x1 -> x0, blocking collectives: 12.9 us -> none  [body(): lax.all_gather(dhidden, 'col', axis=0, tiled=True)]
    dot_general x2 -> x0, local copies, waits for them, and re-layouts: 11.1 us -> none  [the longest x1 5.54 us: body(): jnp.einsum('tij,tif->tjf', values, chosen, preferred_element_type=jnp.flo...]
    unnamed x15, local copies, waits for them, and re-layouts: 0.09 us -> 6.17 us
  transfers between devices with their start and end apart: 8 -> 0, of which waited for: 5 -> 0; matrix products, arithmetic and copies ran while one was open for 3% -> 0% of each run, Pallas kernels for 0% -> 0%
where the time goes in v1:
time: 54.8 us; the launch traced here: 54.5 us
  Pallas kernels  47 us (86%)
  local copies, waits for them, and re-layouts  6.17 us (11%)
  between operations  1.35 us (2%)
    pallas_call x1, Pallas kernels, body(): pl.pallas_call(functools.partial(kernel, rows, cols, reps, fused), out_sh...  47 us
    unnamed x15, local copies, waits for them, and re-layouts  6.17 us

profile of v1, /device:TPU:1, one launch (start us, length us, event | category | flops | bytes accessed | tf_op | source)
XLA Modules:
  0.0 54.5 jit_solution(18061115170368183822)
XLA Ops:
  0.6 0.0 copy-start.5
  0.6 0.0 copy-start.4
  1.3 0.0 copy-done.5
  1.3 0.0 copy-done.4
  1.3 0.0 copy-start
  1.3 1.0 %copy-done = bf16[512,512]{1,0:T(8,128)(2,1)S(1)} copy-done((bf16[512,512]{1,0:T(8,128)(2,1)S(1)}, bf16[512,512]{1,0:T(8,128)(2,1)}, u32[]{:S(2)}) %copy-start) | copy-done | bytes 524312
  2.4 0.0 copy-start.1
  2.4 1.0 %copy-done.1 = bf16[1,16,128,128]{3,2,1,0:T(8,128)(2,1)S(1)} copy-done((bf16[1,16,128,128]{3,2,1,0:T(8,128)(2,1)S(1)}, bf16[1,16,128,128]{3,2,1,0:T(8,128)(2,1)}, u32[]{:S(2)}) %copy-start.1) | copy-done | bytes 524312
  3.4 0.0 copy-start.2
  3.4 0.9 %copy-done.2 = bf16[1,128,512]{2,1,0:T(8,128)(2,1)S(1)} copy-done((bf16[1,128,512]{2,1,0:T(8,128)(2,1)S(1)}, bf16[1,128,512]{2,1,0:T(8,128)(2,1)}, u32[]{:S(2)}) %copy-start.2) | copy-done | bytes 131096
  4.3 0.0 copy-start.3
  4.3 0.9 %copy-done.3 = bf16[1,128,512]{2,1,0:T(8,128)(2,1)S(1)} copy-done((bf16[1,128,512]{2,1,0:T(8,128)(2,1)S(1)}, bf16[1,128,512]{2,1,0:T(8,128)(2,1)}, u32[]{:S(2)}) %copy-start.3) | copy-done | bytes 131096
  5.2 47.0 %shard_map.94 = (bf16[1,128,512]{2,1,0:T(8,128)(2,1)S(1)}, bf16[1,128,512]{2,1,0:T(8,128)(2,1)S(1)}, f32[512,512]{1,0:T(8,128)S(1)}) custom-call(bf16[1,128,512]{2,1,0:T(8,128)(2,1)S(1)} %copy-done.2, bf16[1,128,512]{2,1,0:T(8,128)(2,1)S(1)} %copy-done.3, bf16[512,512]{1,0:T(8,128)(2,1)S(1)} %copy-done, bf16[1,16,128,128]{3,2,1,0:T(8,128)(2,1)S(1)} %copy-done.1, ...), custom_call_target="tpu_custom_call" | custom-call | tf_op jit(solution)/shard_map/pallas_call | solution.py:316
  52.2 0.7 %copy.14 = bf16[1,128,512]{2,1,0:T(8,128)(2,1)} copy(bf16[1,128,512]{2,1,0:T(8,128)(2,1)S(1)} %get-tuple-element.6) | data formatting | bytes 262144
  52.9 0.7 %copy.15 = bf16[1,128,512]{2,1,0:T(8,128)(2,1)} copy(bf16[1,128,512]{2,1,0:T(8,128)(2,1)S(1)} %get-tuple-element.7) | data formatting | bytes 262144
  53.5 1.0 %copy.16 = f32[512,512]{1,0:T(8,128)} copy(f32[512,512]{1,0:T(8,128)S(1)} %get-tuple-element.8) | data formatting | bytes 2097152
Async XLA Ops:
  0.6 0.7 %copy-start.5 = (s32[1,16]{1,0:T(1,128)S(1)}, s32[1,16]{1,0:T(1,128)}, u32[]{:S(2)}) copy-start(s32[1,16]{1,0:T(1,128)} %tins.1) | copy-start | bytes 196
  0.6 0.7 %copy-start.4 = (s32[1,16]{1,0:T(1,128)S(1)}, s32[1,16]{1,0:T(1,128)}, u32[]{:S(2)}) copy-start(s32[1,16]{1,0:T(1,128)} %touts.1) | copy-start | bytes 196
  1.3 1.0 %copy-start = (bf16[512,512]{1,0:T(8,128)(2,1)S(1)}, bf16[512,512]{1,0:T(8,128)(2,1)}, u32[]{:S(2)}) copy-start(bf16[512,512]{1,0:T(8,128)(2,1)} %w.1) | copy-start | bytes 1572868
  2.4 1.0 %copy-start.1 = (bf16[1,16,128,128]{3,2,1,0:T(8,128)(2,1)S(1)}, bf16[1,16,128,128]{3,2,1,0:T(8,128)(2,1)}, u32[]{:S(2)}) copy-start(bf16[1,16,128,128]{3,2,1,0:T(8,128)(2,1)} %vals.1) | copy-start | bytes 1572868
  3.4 0.9 %copy-start.2 = (bf16[1,128,512]{2,1,0:T(8,128)(2,1)S(1)}, bf16[1,128,512]{2,1,0:T(8,128)(2,1)}, u32[]{:S(2)}) copy-start(bf16[1,128,512]{2,1,0:T(8,128)(2,1)} %feat.1) | copy-start | bytes 393220
  4.3 0.9 %copy-start.3 = (bf16[1,128,512]{2,1,0:T(8,128)(2,1)S(1)}, bf16[1,128,512]{2,1,0:T(8,128)(2,1)}, u32[]{:S(2)}) copy-start(bf16[1,128,512]{2,1,0:T(8,128)(2,1)} %cot.1) | copy-start | bytes 393220

commit v2 on v1

--- a/solution.py
+++ b/solution.py
@@ -11,6 +11,24 @@
 HALF = SECTIONS // 2
 OTHERS = tuple(s for s in range(SECTIONS) if s != HALF)
 CHUNKS = 4
+AFTER = (
+    "rep",
+    "spread 1",
+    "adjoint 0",
+    "row",
+    "spread 2",
+    "adjoint 1",
+    "col",
+    "spread 3",
+    "adjoint 2",
+    "back0",
+    "adjoint 3",
+    "back1",
+    "finish 0",
+    "finish 1",
+    "finish 2",
+    "finish 3",
+)
 MESH = pl.DeviceIdType.MESH
 F32, BF16 = jnp.float32, jnp.bfloat16
 
@@ -27,8 +45,10 @@
 
 def kernel(
     rows, cols, reps, fused,
-    feat, cot, w, vals, touts, tins, tcount,
-    out, gfeat, gweight,
+    feat, cot_hbm, w_hbm, vals_hbm, touts, tins, tcount,
+    out_hbm, gfeat_hbm, gweight_hbm,
+    out, gfeat, out_sem, gfeat_sem, gweight_sem,
+    cot, w, vals, feat_sem, cot_sem, w_sem, vals_sem,
     a, at, x, part, arrived, hid, grads, secs, landed,
     mine, rep_in, row_out, row_in, col_out, col_in, full,
     xs, xr, ps, pr, gs, gr, ss, sr, rs, rr, ws, wr, cs, cr, rs2, rr2, ws2, wr2, cs2, cr2,
@@ -56,6 +76,13 @@
     row_peers = ring("row", r, rows) if fused else []
     rep_peers = ring("rep", p, reps) if fused else []
 
+    loads = [pltpu.make_async_copy(feat.at[0, :, cut(j)], x.at[j, sec(HALF), :], feat_sem.at[j]) for j in range(CHUNKS)]
+    vals_load = pltpu.make_async_copy(vals_hbm, vals, vals_sem.at[0])
+    w_load = pltpu.make_async_copy(w_hbm, w, w_sem.at[0])
+    cot_load = pltpu.make_async_copy(cot_hbm, cot, cot_sem.at[0])
+    for load in [vals_load, *loads, w_load, cot_load]:
+        load.start()
+
     barrier = pltpu.get_barrier_semaphore()
     for _, axis, index in col_peers + row_peers + rep_peers:
         pl.semaphore_signal(barrier, inc=1, device_id={axis: index}, device_id_type=MESH)
@@ -80,7 +107,6 @@
                 x_copy(j, n, s).start()
 
     for j in range(CHUNKS):
-        x[j, sec(HALF), :] = feat[0, :, j * wide : (j + 1) * wide]
         for n, s in enumerate(OTHERS):
             @pl.when(jnp.logical_not(inside(r + (s - HALF))))
             def _():
@@ -98,6 +124,7 @@
         for t in range(slots)
     ]
     strip = 16
+    vals_load.wait()
 
     @pl.loop(0, edge // strip)
     def _(step):
@@ -122,12 +149,15 @@
             @pl.when(inside(r + (s - HALF)))
             def _():
                 x_copy(j, n, s).wait_recv()
+        loads[j].wait()
         part[j] = dot(a[...], x[j]).astype(BF16)
         for peer in col_peers:
             part_copy(j, *peer).start()
 
     at[...] = a[...].astype(F32).T.astype(BF16)
 
+    w_load.wait()
+    cot_load.wait()
     pre = jnp.zeros((span, width), F32)
     for j in range(CHUNKS):
         for peer in col_peers:
@@ -149,16 +179,17 @@
         source = pl.ds(pl.multiple_of(lax.rem(c + cols - 1 - k, cols) * span, span), span)
         remote(grads.at[j, source, :], grads.at[j, source, :], gs.at[j, k], gr.at[j, k], "col", col_peers[k][2]).wait_recv()
 
-    for j in range(CHUNKS):
+    def spread(j):
         grads[j, own, :] = dot(dpre, w[j * wide : (j + 1) * wide, :], ((1,), (1,))).astype(BF16)
         for peer in col_peers:
             grad_copy(j, *peer).start()
-    out[0] = (pre * sigma).astype(BF16)
-
+    spread(0)
     scale = float(span * rows * cols * reps) ** -0.5
     term = dot(hid[...].astype(F32).T.astype(BF16), dpre) * scale
     if not fused:
-        gweight[...] = term
+        full[...] = term
+        whole_store = pltpu.make_async_copy(full, gweight_hbm, gweight_sem.at[0])
+        whole_store.start()
     else:
         mine[...] = term.astype(BF16)
         rep_rows = width // reps
@@ -219,7 +250,11 @@
                 sec_copy(j, n, s).wait_recv()
         for n in range(len(OTHERS)):
             total = total + landed[j, n].astype(F32)
-        gfeat[0, :, j * wide : (j + 1) * wide] = total.astype(BF16)
+        gfeat[j] = total.astype(BF16)
+        gfeat_store(j).start()
+
+    def gfeat_store(j):
+        return pltpu.make_async_copy(gfeat.at[j], gfeat_hbm.at[0, :, cut(j)], gfeat_sem.at[j])
 
     def rep_stage():
         for peer in rep_peers:
@@ -257,22 +292,44 @@
         for peer in then:
             back_copy(level + 1, *peer).start()
 
+    def half_store(n, half):
+        return pltpu.make_async_copy(
+            full.at[piece(rep_rows, half), :], gweight_hbm.at[piece(rep_rows, half), :], gweight_sem.at[n]
+        )
+
+    out[0] = (pre * sigma).astype(BF16)
+    out_store = pltpu.make_async_copy(out, out_hbm, out_sem.at[0])
+    out_store.start()
+
+    stages = {
+        "spread": spread,
+        "adjoint": adjoint,
+        "finish": finish,
+        "rep": rep_stage,
+        "row": row_stage,
+        "col": col_stage,
+        "back0": lambda: back_stage(0, col_peers, row_peers),
+        "back1": lambda: back_stage(1, row_peers, rep_peers),
+    }
+    for name in AFTER:
+        stage, _, index = name.partition(" ")
+        if index:
+            stages[stage](int(index))
+        elif fused:
+            stages[stage]()
     if fused:
-        rep_stage()
-    for j in range(CHUNKS):
-        adjoint(j)
-        if fused and j == CHUNKS // 2:
-            row_stage()
+        half_store(0, p).start()
     if fused:
-        col_stage()
-    for j in range(CHUNKS):
-        finish(j)
-        if fused and j == CHUNKS // 2:
-            back_stage(0, col_peers, row_peers)
-    if fused:
-        back_stage(1, row_peers, rep_peers)
         back_stage(2, rep_peers, [])
-        gweight[...] = full[...].astype(F32)
+        for k in range(reps - 1):
+            half_store(k + 1, lax.rem(p + k + 1, reps)).start()
+        for k in range(reps):
+            half_store(k, lax.rem(p + k, reps)).wait()
+    else:
+        whole_store.wait()
+    out_store.wait()
+    for j in range(CHUNKS):
+        gfeat_store(j).wait()
 
     for j in range(CHUNKS):
         for n, s in enumerate(OTHERS):
@@ -310,7 +367,7 @@
         row_rows = rep_rows // rows if fused else 16
         col_rows = row_rows // cols if fused else 16
         few = lambda n: max(1, n - 1)
-        vmem = pl.BlockSpec(memory_space=pltpu.VMEM)
+        hbm = pl.BlockSpec(memory_space=pltpu.HBM)
         smem = pl.BlockSpec(memory_space=pltpu.SMEM)
         sems = lambda *shape: [pltpu.SemaphoreType.DMA(shape)] * 2
         result = pl.pallas_call(
@@ -318,11 +375,23 @@
             out_shape=(
                 jax.ShapeDtypeStruct(feat.shape, BF16),
                 jax.ShapeDtypeStruct(feat.shape, BF16),
-                jax.ShapeDtypeStruct(w.shape, F32),
+                jax.ShapeDtypeStruct(w.shape, BF16 if fused else F32),
             ),
-            in_specs=[vmem] * 4 + [smem] * 3,
-            out_specs=(vmem,) * 3,
+            in_specs=[hbm] * 4 + [smem] * 3,
+            out_specs=(hbm,) * 3,
             scratch_shapes=[
+                pltpu.VMEM(feat.shape, BF16),
+                pltpu.VMEM((CHUNKS, span, wide), BF16),
+                pltpu.SemaphoreType.DMA((1,)),
+                pltpu.SemaphoreType.DMA((CHUNKS,)),
+                pltpu.SemaphoreType.DMA((reps,)),
+                pltpu.VMEM(cot.shape, BF16),
+                pltpu.VMEM(w.shape, BF16),
+                pltpu.VMEM(vals.shape, BF16),
+                pltpu.SemaphoreType.DMA((CHUNKS,)),
+                pltpu.SemaphoreType.DMA((1,)),
+                pltpu.SemaphoreType.DMA((1,)),
+                pltpu.SemaphoreType.DMA((1,)),
                 pltpu.VMEM((cols * edge, SECTIONS * edge), BF16),
                 pltpu.VMEM((SECTIONS * edge, cols * edge), BF16),
                 pltpu.VMEM((CHUNKS, SECTIONS * span, wide), BF16),
@@ -338,7 +407,7 @@
                 pltpu.VMEM((few(rows) if fused else 1, row_rows, width), BF16),
                 pltpu.VMEM((row_rows, width), BF16),
                 pltpu.VMEM((few(cols), col_rows, width), BF16),
-                pltpu.VMEM(w.shape if fused else (16, width), BF16),
+                pltpu.VMEM(w.shape, BF16 if fused else F32),
                 *sems(CHUNKS, len(OTHERS)),
                 *sems(CHUNKS, few(cols)),
                 *sems(CHUNKS, few(cols)),
@@ -346,11 +415,11 @@
                 *(sems(few(reps)) + sems(few(rows) if fused else 1) + sems(few(cols))) * 2,
             ],
             compiler_params=pltpu.CompilerParams(
-                collective_id=0, has_side_effects=True, vmem_limit_bytes=48 * 2**20
+                collective_id=0, has_side_effects=True, vmem_limit_bytes=58 * 2**20
             ),
         )(feat, cot, w, vals, touts, tins, tcount)
         if fused:
-            return result
+            return (*result[:2], result[2].astype(F32))
         return (*result[:2], lax.psum(result[2], ("row", "col", "rep")))
 
     spread = ("row", "col")

time: 54.8 us -> 50 us (0.912)
  local copies, waits for them, and re-layouts: 6.17 us -> 1.61 us
  Pallas kernels: 47 us -> 44.7 us
  other arithmetic: 0 us -> 2.18 us
    unnamed x15 -> x6, local copies, waits for them, and re-layouts: 6.17 us -> 1.61 us
    pallas_call x1, Pallas kernels: 47 us -> 44.7 us  [body(): pl.pallas_call(functools.partial(kernel, rows, cols, reps, fused), out_sh...]
    convert_element_type x0 -> x1, other arithmetic: none -> 2.18 us  [body(): return (*result[:2], result[2].astype(F32))]
where the time goes in v2:
time: 50 us; the launch traced here: 49.8 us
  Pallas kernels  44.7 us (89%)
  other arithmetic  2.18 us (4%)
  local copies, waits for them, and re-layouts  1.61 us (3%)
  between operations  1.3 us (3%)
    pallas_call x1, Pallas kernels, body(): pl.pallas_call(functools.partial(kernel, rows, cols, reps, fused), out_sh...  44.7 us
    convert_element_type x1, other arithmetic, body(): return (*result[:2], result[2].astype(F32))  2.18 us
    unnamed x6, local copies, waits for them, and re-layouts  1.61 us

profile of v2, /device:TPU:1, one launch (start us, length us, event | category | flops | bytes accessed | tf_op | source)
XLA Modules:
  0.0 49.8 jit_solution(2041644059923381250)
XLA Ops:
  1.3 44.7 %shard_map.94 = (bf16[1,128,512]{2,1,0:T(8,128)(2,1)}, bf16[1,128,512]{2,1,0:T(8,128)(2,1)}, bf16[512,512]{1,0:T(8,128)(2,1)}) custom-call(bf16[1,128,512]{2,1,0:T(8,128)(2,1)} %feat.1, bf16[1,128,512]{2,1,0:T(8,128)(2,1)} %cot_hbm.1, bf16[512,512]{1,0:T(8,128)(2,1)} %w_hbm.1, bf16[1,16,128,128]{3,2,1,0:T(8,128)(2,1)} %vals_hbm.1, s32[1,16]{1,0:T(1,128)} %touts.1, ...), custom_call_target="tpu_custom_call" | custom-call | tf_op jit(solution)/shard_map/pallas_call | solution.py:373
  46.0 0.0 copy-start.1
  46.0 2.2 %convert_element_type.3 = f32[512,512]{1,0:T(8,128)} convert(bf16[512,512]{1,0:T(8,128)(2,1)} %get-tuple-element.8) | non-fusion elementwise | flops 262144 | bytes 1572864 | tf_op jit(solution)/shard_map/convert_element_type | solution.py:422
  48.2 0.0 copy-done.1
  48.2 0.0 copy-start
  48.2 0.7 %copy.13 = bf16[1,128,512]{2,1,0:T(8,128)(2,1)} copy(bf16[1,128,512]{2,1,0:T(8,128)(2,1)S(1)} %copy-done.1) | data formatting | bytes 262144
  48.9 0.3 copy-done
  49.2 0.7 %copy.14 = bf16[1,128,512]{2,1,0:T(8,128)(2,1)} copy(bf16[1,128,512]{2,1,0:T(8,128)(2,1)S(1)} %copy-done) | data formatting | bytes 262144
Async XLA Ops:
  46.0 2.2 %copy-start.1 = (bf16[1,128,512]{2,1,0:T(8,128)(2,1)S(1)}, bf16[1,128,512]{2,1,0:T(8,128)(2,1)}, u32[]{:S(2)}) copy-start(bf16[1,128,512]{2,1,0:T(8,128)(2,1)} %get-tuple-element.12) | copy-start | bytes 393220
  48.2 1.0 %copy-start = (bf16[1,128,512]{2,1,0:T(8,128)(2,1)S(1)}, bf16[1,128,512]{2,1,0:T(8,128)(2,1)}, u32[]{:S(2)}) copy-start(bf16[1,128,512]{2,1,0:T(8,128)(2,1)} %get-tuple-element.13) | copy-start | bytes 393220
